TPU v7x, 32 devices: a whole 2x2x4 slice. The times are simulated.
32 devices in a mesh: row: 4 (over z), col: 4 (over y, x), depth: 2 (over core).
Axes of the slice: x: 2, y: 2, z: 4, core: 2. Of those that a mesh axis runs over, the one named last changes fastest.
Arguments:
- density: bfloat16 [2048, 2048], P('row', 'col'), may hold values from -1 to 1, as said below
- pattern: int32 [8, 8], replicated, may hold values from 0 to 1, as said below
- filter_pattern: int32 [8, 8], replicated, may hold values from 0 to 1, as said below
Outputs:
- square: bfloat16 [2048, 2048], P(('row', 'depth'), 'col')
Inputs may be any that keep to these rules, and one draw needn't show every extreme that they name: density equals its transpose. 1 marks a stored block; the pattern is symmetric and every diagonal block is stored. `filter_pattern`: 1 marks a block that is kept; the pattern is symmetric and every diagonal block is kept.
All inputs are finite; a program needn't handle non-finite values.
Results may differ from a plain program's by a relative error of at most 0.001.
Values may be sent and summed in bfloat16 or wider, within the bound.
A program may use at most 64 MiB of HBM per device.

v0:
```python
import jax
import jax.numpy as jnp
from jax import lax
from jax.sharding import PartitionSpec as P

BS = 256


def shifted(value, axis, steps):
    count = lax.axis_size(axis)
    pairs = [(source, (source + steps) % count) for source in range(count)]
    return lax.ppermute(value, axis, pairs)


def apply_mask(values, block_mask, zero_value):
    row_blocks, col_blocks = block_mask.shape
    shaped = values.reshape(row_blocks, BS, col_blocks, BS)
    kept = block_mask[:, None, :, None] == 1
    return jnp.where(kept, shaped, zero_value).reshape(values.shape)


def align_left(values, amount, grid_size):
    for bit_index in range(grid_size.bit_length() - 1):
        moved = shifted(values, "col", -(1 << bit_index))
        values = jnp.where(amount >> bit_index & 1 == 1, moved, values)
    return values


def align_right(values, amount, grid_size):
    for bit_index in range(grid_size.bit_length() - 1):
        moved = shifted(values, "row", -(1 << bit_index))
        values = jnp.where(amount >> bit_index & 1 == 1, moved, values)
    return values


def local(density, pattern, filter_pattern):
    grid_size = lax.axis_size("row")
    layer_count = lax.axis_size("depth")
    row_index = lax.axis_index("row")
    col_index = lax.axis_index("col")
    layer_index = lax.axis_index("depth")
    tile_blocks = density.shape[0] // BS
    half_blocks = tile_blocks // layer_count
    own_mask = lax.dynamic_slice(
        pattern, (row_index * tile_blocks, col_index * tile_blocks), (tile_blocks, tile_blocks)
    )
    own_tile = apply_mask(density, own_mask, jnp.zeros((), jnp.bfloat16))
    left_tile = lax.dynamic_slice_in_dim(
        own_tile, layer_index * half_blocks * BS, half_blocks * BS, 0
    )
    left_tile = align_left(left_tile, row_index % grid_size, grid_size)
    right_tile = align_right(own_tile, col_index % grid_size, grid_size)

    def multiply(partial_value, left_cur, right_cur):
        return partial_value + jnp.dot(left_cur, right_cur, preferred_element_type=jnp.float32)

    def advance(step_index, carry):
        partial_value, left_cur, right_cur = carry
        partial_value = multiply(partial_value, left_cur, right_cur)
        left_cur = shifted(left_cur, "col", -1)
        right_cur = shifted(right_cur, "row", -1)
        return (partial_value, left_cur, right_cur)

    start = jnp.zeros((half_blocks * BS, tile_blocks * BS), jnp.float32)
    partial_value, left_cur, right_cur = lax.fori_loop(
        0, grid_size - 1, advance, (start, left_tile, right_tile)
    )
    partial_value = multiply(partial_value, left_cur, right_cur)
    out_row0 = row_index * tile_blocks + layer_index * half_blocks
    keep_mask = lax.dynamic_slice(
        filter_pattern, (out_row0, col_index * tile_blocks), (half_blocks, tile_blocks)
    )
    return apply_mask(partial_value, keep_mask, jnp.zeros((), jnp.float32)).astype(jnp.bfloat16)


def solution(mesh):
    return jax.shard_map(
        local,
        mesh=mesh,
        in_specs=(P("row", "col"), P(), P()),
        out_specs=P(("row", "depth"), "col"),
        check_vma=False,
    )
```

profile of v0, /device:TPU:0, one launch (start us, length us, event | category | flops | bytes accessed | tf_op | source)
XLA Modules:
  0.0 87.4 jit_solution(5741546577819286075)
XLA Ops:
  0.0 0.8 dynamic-slice_compare_fusion
  1.3 0.9 %copy-done = bf16[512,512]{1,0:T(8,128)(2,1)S(1)} copy-done((bf16[512,512]{1,0:T(8,128)(2,1)S(1)}, bf16[512,512]{1,0:T(8,128)(2,1)}, u32[]{:S(2)}) %copy-start) | copy-done | bytes 524312
  2.2 5.1 %collective-permute-start.4 = (bf16[512,512]{1,0:T(8,128)(2,1)S(1)}, bf16[512,512]{1,0:T(8,128)(2,1)S(1)}, u32[]{:S(2)}, u32[]{:S(2)}) collective-permute-start(bf16[512,512]{1,0:T(8,128)(2,1)S(1)} %broadcast_select_fusion.2), channel_id=1, source_target_pairs={{0,24},{8,0},{16,8},{24,16},{1,25},{9,1},{17,9},{25,17},{2,26},{10... | collective-permute-start | bytes 1572872 | tf_op jit(solution)/shard_map/ppermute | solution.py:12
  7.3 2.5 %collective-permute-start.2 = (bf16[256,512]{1,0:T(8,128)(2,1)S(1)}, bf16[256,512]{1,0:T(8,128)(2,1)S(1)}, u32[]{:S(2)}, u32[]{:S(2)}) collective-permute-start(bf16[256,512]{1,0:T(8,128)(2,1)S(1)} %constant_dynamic-slice_fusion), channel_id=1, source_target_pairs={{0,6},{2,0},{4,2},{6,4},{1,7},{3,1},{5,3},{7,5},{8,14},{10,8},{12,... | collective-permute-start | bytes 786440 | tf_op jit(solution)/shard_map/ppermute | solution.py:12
  9.8 8.7 %collective-permute-done.4 = bf16[512,512]{1,0:T(8,128)(2,1)S(1)} collective-permute-done((bf16[512,512]{1,0:T(8,128)(2,1)S(1)}, bf16[512,512]{1,0:T(8,128)(2,1)S(1)}, u32[]{:S(2)}, u32[]{:S(2)}) %collective-permute-start.4) | collective-permute-done | bytes 524320 | tf_op jit(solution)/shard_map/ppermute | solution.py:12
  18.6 1.5 %collective-permute-start.5 = (bf16[512,512]{1,0:T(8,128)(2,1)S(1)}, bf16[512,512]{1,0:T(8,128)(2,1)S(1)}, u32[]{:S(2)}, u32[]{:S(2)}) collective-permute-start(bf16[512,512]{1,0:T(8,128)(2,1)S(1)} %broadcast_select_fusion), channel_id=1, source_target_pairs={{0,16},{8,24},{16,0},{24,8},{1,17},{9,25},{17,1},{25,9},{2,18},{10... | collective-permute-start | bytes 1572872 | tf_op jit(solution)/shard_map/ppermute | solution.py:12
  20.2 1.6 %collective-permute-start.3 = (bf16[256,512]{1,0:T(8,128)(2,1)S(1)}, bf16[256,512]{1,0:T(8,128)(2,1)S(1)}, u32[]{:S(2)}, u32[]{:S(2)}) collective-permute-start(bf16[256,512]{1,0:T(8,128)(2,1)S(1)} %broadcast_select_fusion.3), channel_id=1, source_target_pairs={{0,4},{2,6},{4,0},{6,2},{1,5},{3,7},{5,1},{7,3},{8,12},{10,14},{12... | collective-permute-start | bytes 786440 | tf_op jit(solution)/shard_map/ppermute | solution.py:12
  21.8 0.8 compare_bitcast_fusion
  22.6 4.5 %collective-permute-done.3 = bf16[256,512]{1,0:T(8,128)(2,1)S(1)} collective-permute-done((bf16[256,512]{1,0:T(8,128)(2,1)S(1)}, bf16[256,512]{1,0:T(8,128)(2,1)S(1)}, u32[]{:S(2)}, u32[]{:S(2)}) %collective-permute-start.3) | collective-permute-done | bytes 262176 | tf_op jit(solution)/shard_map/ppermute | solution.py:12
  27.2 16.4 %collective-permute-done.5 = bf16[512,512]{1,0:T(8,128)(2,1)S(1)} collective-permute-done((bf16[512,512]{1,0:T(8,128)(2,1)S(1)}, bf16[512,512]{1,0:T(8,128)(2,1)S(1)}, u32[]{:S(2)}, u32[]{:S(2)}) %collective-permute-start.5) | collective-permute-done | bytes 524320 | tf_op jit(solution)/shard_map/ppermute | solution.py:12
  43.6 42.7 %while.15 = (s32[]{:T(128)}, f32[256,512]{1,0:T(8,128)S(1)}, bf16[256,512]{1,0:T(8,128)(2,1)S(1)}, bf16[512,512]{1,0:T(8,128)(2,1)S(1)}, s32[]{:T(128)}, /*index=5*/s32[]{:T(128)}) while((s32[]{:T(128)}, f32[256,512]{1,0:T(8,128)S(1)}, bf16[256,512]{1,0:T(8,128)(2,1)S(1)}, bf16[512,512]{1,0:T(8,128)(2,1)S(1)}, s32[]{:T(128)}, ...), condition=%wide.region_1.2_spmd.clone, body=%wide.region_0.1_spmd.clone.sunk | while | flops 134479872 | bytes 6553759 | solution.py:65
  43.7 2.4 %collective-permute-start.1 = (bf16[512,512]{1,0:T(8,128)(2,1)S(1)}, bf16[512,512]{1,0:T(8,128)(2,1)S(1)}, u32[]{:S(2)}, u32[]{:S(2)}) collective-permute-start(bf16[512,512]{1,0:T(8,128)(2,1)S(1)} %copy.12), channel_id=1, source_target_pairs={{0,24},{8,0},{16,8},{24,16},{1,25},{9,1},{17,9},{25,17},{2,26},{10... | collective-permute-start | bytes 1572872 | tf_op jit(solution)/shard_map/while/body/eval_jaxpr/ppermute | solution.py:12
  46.1 2.5 %collective-permute-start = (bf16[256,512]{1,0:T(8,128)(2,1)S(1)}, bf16[256,512]{1,0:T(8,128)(2,1)S(1)}, u32[]{:S(2)}, u32[]{:S(2)}) collective-permute-start(bf16[256,512]{1,0:T(8,128)(2,1)S(1)} %copy.11), channel_id=1, source_target_pairs={{0,6},{2,0},{4,2},{6,4},{1,7},{3,1},{5,3},{7,5},{8,14},{10,8},{12,... | collective-permute-start | bytes 786440 | tf_op jit(solution)/shard_map/while/body/eval_jaxpr/ppermute | solution.py:12
  49.0 5.1 %collective-permute-done = bf16[256,512]{1,0:T(8,128)(2,1)S(1)} collective-permute-done((bf16[256,512]{1,0:T(8,128)(2,1)S(1)}, bf16[256,512]{1,0:T(8,128)(2,1)S(1)}, u32[]{:S(2)}, u32[]{:S(2)}) %collective-permute-start) | collective-permute-done | bytes 262176 | tf_op jit(solution)/shard_map/while/body/eval_jaxpr/ppermute | solution.py:12
  54.1 3.3 %collective-permute-done.1 = bf16[512,512]{1,0:T(8,128)(2,1)S(1)} collective-permute-done((bf16[512,512]{1,0:T(8,128)(2,1)S(1)}, bf16[512,512]{1,0:T(8,128)(2,1)S(1)}, u32[]{:S(2)}, u32[]{:S(2)}) %collective-permute-start.1) | collective-permute-done | bytes 524320 | tf_op jit(solution)/shard_map/while/body/eval_jaxpr/ppermute | solution.py:12
  57.5 4.3 %collective-permute-start.1 = (bf16[512,512]{1,0:T(8,128)(2,1)S(1)}, bf16[512,512]{1,0:T(8,128)(2,1)S(1)}, u32[]{:S(2)}, u32[]{:S(2)}) collective-permute-start(bf16[512,512]{1,0:T(8,128)(2,1)S(1)} %copy.12), channel_id=1, source_target_pairs={{0,24},{8,0},{16,8},{24,16},{1,25},{9,1},{17,9},{25,17},{2,26},{10... | collective-permute-start | bytes 1572872 | tf_op jit(solution)/shard_map/while/body/eval_jaxpr/ppermute | solution.py:12
  61.8 2.5 %collective-permute-start = (bf16[256,512]{1,0:T(8,128)(2,1)S(1)}, bf16[256,512]{1,0:T(8,128)(2,1)S(1)}, u32[]{:S(2)}, u32[]{:S(2)}) collective-permute-start(bf16[256,512]{1,0:T(8,128)(2,1)S(1)} %copy.11), channel_id=1, source_target_pairs={{0,6},{2,0},{4,2},{6,4},{1,7},{3,1},{5,3},{7,5},{8,14},{10,8},{12,... | collective-permute-start | bytes 786440 | tf_op jit(solution)/shard_map/while/body/eval_jaxpr/ppermute | solution.py:12
  64.7 4.3 %collective-permute-done = bf16[256,512]{1,0:T(8,128)(2,1)S(1)} collective-permute-done((bf16[256,512]{1,0:T(8,128)(2,1)S(1)}, bf16[256,512]{1,0:T(8,128)(2,1)S(1)}, u32[]{:S(2)}, u32[]{:S(2)}) %collective-permute-start) | collective-permute-done | bytes 262176 | tf_op jit(solution)/shard_map/while/body/eval_jaxpr/ppermute | solution.py:12
  69.0 3.3 %collective-permute-done.1 = bf16[512,512]{1,0:T(8,128)(2,1)S(1)} collective-permute-done((bf16[512,512]{1,0:T(8,128)(2,1)S(1)}, bf16[512,512]{1,0:T(8,128)(2,1)S(1)}, u32[]{:S(2)}, u32[]{:S(2)}) %collective-permute-start.1) | collective-permute-done | bytes 524320 | tf_op jit(solution)/shard_map/while/body/eval_jaxpr/ppermute | solution.py:12
  72.4 4.3 %collective-permute-start.1 = (bf16[512,512]{1,0:T(8,128)(2,1)S(1)}, bf16[512,512]{1,0:T(8,128)(2,1)S(1)}, u32[]{:S(2)}, u32[]{:S(2)}) collective-permute-start(bf16[512,512]{1,0:T(8,128)(2,1)S(1)} %copy.12), channel_id=1, source_target_pairs={{0,24},{8,0},{16,8},{24,16},{1,25},{9,1},{17,9},{25,17},{2,26},{10... | collective-permute-start | bytes 1572872 | tf_op jit(solution)/shard_map/while/body/eval_jaxpr/ppermute | solution.py:12
  76.7 2.5 %collective-permute-start = (bf16[256,512]{1,0:T(8,128)(2,1)S(1)}, bf16[256,512]{1,0:T(8,128)(2,1)S(1)}, u32[]{:S(2)}, u32[]{:S(2)}) collective-permute-start(bf16[256,512]{1,0:T(8,128)(2,1)S(1)} %copy.11), channel_id=1, source_target_pairs={{0,6},{2,0},{4,2},{6,4},{1,7},{3,1},{5,3},{7,5},{8,14},{10,8},{12,... | collective-permute-start | bytes 786440 | tf_op jit(solution)/shard_map/while/body/eval_jaxpr/ppermute | solution.py:12
  79.6 3.6 %collective-permute-done = bf16[256,512]{1,0:T(8,128)(2,1)S(1)} collective-permute-done((bf16[256,512]{1,0:T(8,128)(2,1)S(1)}, bf16[256,512]{1,0:T(8,128)(2,1)S(1)}, u32[]{:S(2)}, u32[]{:S(2)}) %collective-permute-start) | collective-permute-done | bytes 262176 | tf_op jit(solution)/shard_map/while/body/eval_jaxpr/ppermute | solution.py:12
  83.2 3.2 %collective-permute-done.1 = bf16[512,512]{1,0:T(8,128)(2,1)S(1)} collective-permute-done((bf16[512,512]{1,0:T(8,128)(2,1)S(1)}, bf16[512,512]{1,0:T(8,128)(2,1)S(1)}, u32[]{:S(2)}, u32[]{:S(2)}) %collective-permute-start.1) | collective-permute-done | bytes 524320 | tf_op jit(solution)/shard_map/while/body/eval_jaxpr/ppermute | solution.py:12
  86.6 0.8 select_convert_fusion
  (23 shorter events, 2.4 us)
Async XLA Ops:
  1.1 1.0 %copy-start = (bf16[512,512]{1,0:T(8,128)(2,1)S(1)}, bf16[512,512]{1,0:T(8,128)(2,1)}, u32[]{:S(2)}) copy-start(bf16[512,512]{1,0:T(8,128)(2,1)} %param.5) | copy-start | bytes 1572868
  2.2 16.3 %collective-permute-start.4 = (bf16[512,512]{1,0:T(8,128)(2,1)S(1)}, bf16[512,512]{1,0:T(8,128)(2,1)S(1)}, u32[]{:S(2)}, u32[]{:S(2)}) collective-permute-start(bf16[512,512]{1,0:T(8,128)(2,1)S(1)} %broadcast_select_fusion.2), channel_id=1, source_target_pairs={{0,24},{8,0},{16,8},{24,16},{1,25},{9,1},{17,9},{25,17},{2,26},{10... | collective-permute-start | bytes 1572872 | tf_op jit(solution)/shard_map/ppermute | solution.py:12
  7.3 12.8 %collective-permute-start.2 = (bf16[256,512]{1,0:T(8,128)(2,1)S(1)}, bf16[256,512]{1,0:T(8,128)(2,1)S(1)}, u32[]{:S(2)}, u32[]{:S(2)}) collective-permute-start(bf16[256,512]{1,0:T(8,128)(2,1)S(1)} %constant_dynamic-slice_fusion), channel_id=1, source_target_pairs={{0,6},{2,0},{4,2},{6,4},{1,7},{3,1},{5,3},{7,5},{8,14},{10,8},{12,... | collective-permute-start | bytes 786440 | tf_op jit(solution)/shard_map/ppermute | solution.py:12
  18.6 25.0 %collective-permute-start.5 = (bf16[512,512]{1,0:T(8,128)(2,1)S(1)}, bf16[512,512]{1,0:T(8,128)(2,1)S(1)}, u32[]{:S(2)}, u32[]{:S(2)}) collective-permute-start(bf16[512,512]{1,0:T(8,128)(2,1)S(1)} %broadcast_select_fusion), channel_id=1, source_target_pairs={{0,16},{8,24},{16,0},{24,8},{1,17},{9,25},{17,1},{25,9},{2,18},{10... | collective-permute-start | bytes 1572872 | tf_op jit(solution)/shard_map/ppermute | solution.py:12
  20.2 7.0 %collective-permute-start.3 = (bf16[256,512]{1,0:T(8,128)(2,1)S(1)}, bf16[256,512]{1,0:T(8,128)(2,1)S(1)}, u32[]{:S(2)}, u32[]{:S(2)}) collective-permute-start(bf16[256,512]{1,0:T(8,128)(2,1)S(1)} %broadcast_select_fusion.3), channel_id=1, source_target_pairs={{0,4},{2,6},{4,0},{6,2},{1,5},{3,7},{5,1},{7,3},{8,12},{10,14},{12... | collective-permute-start | bytes 786440 | tf_op jit(solution)/shard_map/ppermute | solution.py:12
  43.7 13.8 %collective-permute-start.1 = (bf16[512,512]{1,0:T(8,128)(2,1)S(1)}, bf16[512,512]{1,0:T(8,128)(2,1)S(1)}, u32[]{:S(2)}, u32[]{:S(2)}) collective-permute-start(bf16[512,512]{1,0:T(8,128)(2,1)S(1)} %copy.12), channel_id=1, source_target_pairs={{0,24},{8,0},{16,8},{24,16},{1,25},{9,1},{17,9},{25,17},{2,26},{10... | collective-permute-start | bytes 1572872 | tf_op jit(solution)/shard_map/while/body/eval_jaxpr/ppermute | solution.py:12
  46.1 8.0 %collective-permute-start = (bf16[256,512]{1,0:T(8,128)(2,1)S(1)}, bf16[256,512]{1,0:T(8,128)(2,1)S(1)}, u32[]{:S(2)}, u32[]{:S(2)}) collective-permute-start(bf16[256,512]{1,0:T(8,128)(2,1)S(1)} %copy.11), channel_id=1, source_target_pairs={{0,6},{2,0},{4,2},{6,4},{1,7},{3,1},{5,3},{7,5},{8,14},{10,8},{12,... | collective-permute-start | bytes 786440 | tf_op jit(solution)/shard_map/while/body/eval_jaxpr/ppermute | solution.py:12
  57.5 14.9 %collective-permute-start.1 = (bf16[512,512]{1,0:T(8,128)(2,1)S(1)}, bf16[512,512]{1,0:T(8,128)(2,1)S(1)}, u32[]{:S(2)}, u32[]{:S(2)}) collective-permute-start(bf16[512,512]{1,0:T(8,128)(2,1)S(1)} %copy.12), channel_id=1, source_target_pairs={{0,24},{8,0},{16,8},{24,16},{1,25},{9,1},{17,9},{25,17},{2,26},{10... | collective-permute-start | bytes 1572872 | tf_op jit(solution)/shard_map/while/body/eval_jaxpr/ppermute | solution.py:12
  61.8 7.2 %collective-permute-start = (bf16[256,512]{1,0:T(8,128)(2,1)S(1)}, bf16[256,512]{1,0:T(8,128)(2,1)S(1)}, u32[]{:S(2)}, u32[]{:S(2)}) collective-permute-start(bf16[256,512]{1,0:T(8,128)(2,1)S(1)} %copy.11), channel_id=1, source_target_pairs={{0,6},{2,0},{4,2},{6,4},{1,7},{3,1},{5,3},{7,5},{8,14},{10,8},{12,... | collective-permute-start | bytes 786440 | tf_op jit(solution)/shard_map/while/body/eval_jaxpr/ppermute | solution.py:12
  72.4 13.9 %collective-permute-start.1 = (bf16[512,512]{1,0:T(8,128)(2,1)S(1)}, bf16[512,512]{1,0:T(8,128)(2,1)S(1)}, u32[]{:S(2)}, u32[]{:S(2)}) collective-permute-start(bf16[512,512]{1,0:T(8,128)(2,1)S(1)} %copy.12), channel_id=1, source_target_pairs={{0,24},{8,0},{16,8},{24,16},{1,25},{9,1},{17,9},{25,17},{2,26},{10... | collective-permute-start | bytes 1572872 | tf_op jit(solution)/shard_map/while/body/eval_jaxpr/ppermute | solution.py:12
  76.7 6.4 %collective-permute-start = (bf16[256,512]{1,0:T(8,128)(2,1)S(1)}, bf16[256,512]{1,0:T(8,128)(2,1)S(1)}, u32[]{:S(2)}, u32[]{:S(2)}) collective-permute-start(bf16[256,512]{1,0:T(8,128)(2,1)S(1)} %copy.11), channel_id=1, source_target_pairs={{0,6},{2,0},{4,2},{6,4},{1,7},{3,1},{5,3},{7,5},{8,14},{10,8},{12,... | collective-permute-start | bytes 786440 | tf_op jit(solution)/shard_map/while/body/eval_jaxpr/ppermute | solution.py:12
where the time goes:
time: 87.6 us; the launch traced here: 87.4 us
  waiting for transfers between devices  52.4 us (60%)
  starting transfers between devices  29.3 us (33%)
  other arithmetic  2.62 us (3%)
  local copies, waits for them, and re-layouts  1.64 us (2%)
  matrix products  1.37 us (2%)
    ppermute x10, waiting for transfers between devices, shifted(): return lax.ppermute(value, axis, pairs)  52.4 us
    ppermute x10, starting transfers between devices, shifted(): return lax.ppermute(value, axis, pairs)  29.3 us
  transfers between devices with their start and end apart: 10, of which 9 were waited for; matrix products, arithmetic and copies ran while one was open for 2% of the time, Pallas kernels for 0%

commit v1 on v0

v1 whole, which is shorter than its diff:
```python
import functools

import jax
import jax.numpy as jnp
from jax import lax
from jax.experimental import pallas as pl
from jax.experimental.pallas import tpu as pltpu
from jax.sharding import PartitionSpec as P

BS = 256
PIECES = 2
MESH = pl.DeviceIdType.MESH


def kernel(grid, density, pattern, keep, out, left, right, total, *sems):
    (left_send, left_recv, up_send, down_send, right_recv, sib_send, sib_recv) = sems
    row = lax.axis_index("row")
    col = lax.axis_index("col")
    layer = lax.axis_index("depth")
    other = 1 - layer
    tile = density.shape[0]
    blocks = tile // BS
    half = tile // 2
    half_blocks = half // BS
    piece = half // PIECES

    barrier = pltpu.get_barrier_semaphore()

    def greet(device):
        pl.semaphore_signal(barrier, inc=1, device_id=device, device_id_type=MESH)

    for step in range(1, grid):
        greet((row, lax.rem(col + step, grid), layer))
    greet((row, col, other))

    @pl.when(row > 0)
    def _():
        greet((row - 1, col, layer))

    @pl.when(row < grid - 1)
    def _():
        greet((row + 1, col, layer))

    for i in range(blocks):
        for j in range(blocks):
            stored = pattern[row * blocks + i, col * blocks + j] == 1
            block = density[i * BS:(i + 1) * BS, j * BS:(j + 1) * BS]
            side, at = divmod(i, half_blocks)
            right[row, side, at * BS:(at + 1) * BS, j * BS:(j + 1) * BS] = jnp.where(
                stored, block, jnp.zeros_like(block)
            )

    ends = (row > 0).astype(jnp.int32) + (row < grid - 1).astype(jnp.int32)
    pl.semaphore_wait(barrier, grid + ends)

    def part(k, side, p):
        return right.at[k, side, pl.ds(p * piece, piece)]

    def upward(k, p):
        return pltpu.make_async_remote_copy(
            part(k, layer, p), part(k, layer, p), up_send.at[k, p], right_recv.at[k, p],
            device_id=(row + 1, col, layer), device_id_type=MESH,
        )

    def downward(k, p):
        return pltpu.make_async_remote_copy(
            part(k, layer, p), part(k, layer, p), down_send.at[k, p], right_recv.at[k, p],
            device_id=(row - 1, col, layer), device_id_type=MESH,
        )

    def across(k, p):
        return pltpu.make_async_remote_copy(
            part(k, layer, p), part(k, layer, p), sib_send.at[k, p], sib_recv.at[k, p],
            device_id=(row, col, other), device_id_type=MESH,
        )

    def from_across(k, p):
        return pltpu.make_async_remote_copy(
            part(k, other, p), part(k, other, p), sib_send.at[k, p], sib_recv.at[k, p],
            device_id=(row, col, other), device_id_type=MESH,
        )

    def along(step, slot):
        return pltpu.make_async_remote_copy(
            right.at[row, layer], left.at[slot], left_send.at[step], left_recv.at[slot],
            device_id=(row, lax.rem(col + step, grid), layer), device_id_type=MESH,
        )

    for p in range(PIECES):
        @pl.when(row < grid - 1)
        def _():
            upward(row, p).start()

        @pl.when(row > 0)
        def _():
            downward(row, p).start()

    for step in range(1, grid):
        along(step, col).start()

    left[col] = right[row, layer]

    total[...] = jnp.zeros_like(total)

    def multiply(k, remote):
        @pl.when(k != col)
        def _():
            along(0, k).wait_recv()

        if remote:
            for p in range(PIECES):
                from_across(k, p).wait_recv()
        for side in range(2):
            total[...] += jnp.dot(
                left[k, :, side * half:(side + 1) * half],
                right[k, side],
                preferred_element_type=jnp.float32,
            )

    def pass_on(step):
        for p in range(PIECES):
            @pl.when(row - step >= 0)
            def _():
                k = row - step
                upward(k, p).wait_recv()

                @pl.when(row < grid - 1)
                def _():
                    upward(k, p).start()

                across(k, p).start()

            @pl.when(row + step < grid)
            def _():
                k = row + step
                downward(k, p).wait_recv()

                @pl.when(row > 0)
                def _():
                    downward(k, p).start()

                across(k, p).start()

    def multiply_step(step):
        if step == 0:
            multiply(row, False)
            return

        @pl.when(row - step >= 0)
        def _():
            multiply(row - step, True)

        @pl.when(row + step < grid)
        def _():
            multiply(row + step, True)

    for step in range(1, grid):
        pass_on(step)
        multiply_step(step - 1)
    multiply_step(grid - 1)

    for i in range(half_blocks):
        for j in range(blocks):
            kept = keep[row * blocks + layer * half_blocks + i, col * blocks + j] == 1
            rows, cols = slice(i * BS, (i + 1) * BS), slice(j * BS, (j + 1) * BS)
            value = total[rows, cols]
            out[rows, cols] = jnp.where(kept, value, jnp.zeros_like(value)).astype(out.dtype)

    for step in range(1, grid):
        along(step, col).wait_send()
    for k in range(grid):
        for p in range(PIECES):
            @pl.when((row < grid - 1) & (k <= row))
            def _():
                upward(k, p).wait_send()

            @pl.when((row > 0) & (k >= row))
            def _():
                downward(k, p).wait_send()

            @pl.when(k != row)
            def _():
                across(k, p).wait_send()


def local(density, pattern, filter_pattern):
    grid = lax.axis_size("row")
    tile = density.shape[0]
    half = tile // 2
    dma = pltpu.SemaphoreType.DMA
    return pl.pallas_call(
        functools.partial(kernel, grid),
        out_shape=jax.ShapeDtypeStruct((half, tile), jnp.bfloat16),
        in_specs=[
            pl.BlockSpec(memory_space=pltpu.VMEM),
            pl.BlockSpec(memory_space=pltpu.SMEM),
            pl.BlockSpec(memory_space=pltpu.SMEM),
        ],
        out_specs=pl.BlockSpec(memory_space=pltpu.VMEM),
        scratch_shapes=[
            pltpu.VMEM((grid, half, tile), jnp.bfloat16),
            pltpu.VMEM((grid, 2, half, tile), jnp.bfloat16),
            pltpu.VMEM((half, tile), jnp.float32),
            dma((grid,)),
            dma((grid,)),
            dma((grid, PIECES)),
            dma((grid, PIECES)),
            dma((grid, PIECES)),
            dma((grid, PIECES)),
            dma((grid, PIECES)),
        ],
        compiler_params=pltpu.CompilerParams(
            collective_id=0, has_side_effects=True, vmem_limit_bytes=40 * 1024 * 1024
        ),
    )(density, pattern, filter_pattern)


def solution(mesh):
    return jax.shard_map(
        local,
        mesh=mesh,
        in_specs=(P("row", "col"), P(), P()),
        out_specs=P(("row", "depth"), "col"),
        check_vma=False,
    )
```

time: 87.6 us -> 29.3 us (0.33)
  waiting for transfers between devices: 52.4 us -> 0 us
  starting transfers between devices: 29.3 us -> 0 us
  Pallas kernels: 0 us -> 25.7 us
  other arithmetic: 2.62 us -> 0 us
  local copies, waits for them, and re-layouts: 1.64 us -> 3.12 us
  matrix products: 1.37 us -> 0 us
    ppermute x10 -> x0, waiting for transfers between devices: 52.4 us -> none  [shifted(): return lax.ppermute(value, axis, pairs)]
    ppermute x10 -> x0, starting transfers between devices: 29.3 us -> none  [shifted(): return lax.ppermute(value, axis, pairs)]
    pallas_call x0 -> x1, Pallas kernels: none -> 25.7 us  [local(): pl.pallas_call(functools.partial(kernel, grid), out_shape=jax.ShapeDtypeS...]
    unnamed x3 -> x7, local copies, waits for them, and re-layouts: 1.03 us -> 3.12 us
    eq x2 -> x0, other arithmetic: 1.52 us -> none  [apply_mask(): kept = block_mask[:, None, :, None] == 1]
    dot_general x4 -> x0, matrix products: 1.37 us -> none  [multiply(): jnp.dot(left_cur, right_cur, preferred_element_type=jnp.float32)]
  transfers between devices with their start and end apart: 10 -> 0, of which waited for: 9 -> 0; matrix products, arithmetic and copies ran while one was open for 2% -> 0% of each run, Pallas kernels for 0% -> 0%
where the time goes in v1:
time: 29.3 us; the launch traced here: 28.8 us
  Pallas kernels  25.7 us (88%)
  local copies, waits for them, and re-layouts  3.12 us (11%)
    pallas_call x1, Pallas kernels, local(): pl.pallas_call(functools.partial(kernel, grid), out_shape=jax.ShapeDtypeS...  25.7 us
    unnamed x7, local copies, waits for them, and re-layouts  3.12 us

profile of v1, /device:TPU:0, one launch (start us, length us, event | category | flops | bytes accessed | tf_op | source)
XLA Modules:
  0.0 28.8 jit_solution(12320566525247513571)
XLA Ops:
  0.0 0.0 copy-start
  0.0 1.0 %copy-done = bf16[512,512]{1,0:T(8,128)(2,1)S(1)} copy-done((bf16[512,512]{1,0:T(8,128)(2,1)S(1)}, bf16[512,512]{1,0:T(8,128)(2,1)}, u32[]{:S(2)}) %copy-start) | copy-done | bytes 524312
  1.0 0.0 copy-start.1
  1.0 0.7 %copy-done.1 = s32[8,8]{1,0:T(8,128)S(1)} copy-done((s32[8,8]{1,0:T(8,128)S(1)}, s32[8,8]{1,0:T(8,128)}, u32[]{:S(2)}) %copy-start.1) | copy-done | bytes 280
  1.7 0.0 copy-start.2
  1.7 0.7 %copy-done.2 = s32[8,8]{1,0:T(8,128)S(1)} copy-done((s32[8,8]{1,0:T(8,128)S(1)}, s32[8,8]{1,0:T(8,128)}, u32[]{:S(2)}) %copy-start.2) | copy-done | bytes 280
  2.4 25.7 %shard_map.37 = bf16[256,512]{1,0:T(8,128)(2,1)S(1)} custom-call(bf16[512,512]{1,0:T(8,128)(2,1)S(1)} %copy-done, s32[8,8]{1,0:T(8,128)S(1)} %copy-done.1, s32[8,8]{1,0:T(8,128)S(1)} %copy-done.2), custom_call_target="tpu_custom_call" | custom-call | tf_op jit(solution)/shard_map/pallas_call | solution.py:191
  28.1 0.7 %copy.5 = bf16[256,512]{1,0:T(8,128)(2,1)} copy(bf16[256,512]{1,0:T(8,128)(2,1)S(1)} %shard_map.37) | data formatting | bytes 524288
Async XLA Ops:
  0.0 1.0 %copy-start = (bf16[512,512]{1,0:T(8,128)(2,1)S(1)}, bf16[512,512]{1,0:T(8,128)(2,1)}, u32[]{:S(2)}) copy-start(bf16[512,512]{1,0:T(8,128)(2,1)} %density.1) | copy-start | bytes 1572868
  1.0 0.7 %copy-start.1 = (s32[8,8]{1,0:T(8,128)S(1)}, s32[8,8]{1,0:T(8,128)}, u32[]{:S(2)}) copy-start(s32[8,8]{1,0:T(8,128)} %pattern.1) | copy-start | bytes 772
  1.7 0.7 %copy-start.2 = (s32[8,8]{1,0:T(8,128)S(1)}, s32[8,8]{1,0:T(8,128)}, u32[]{:S(2)}) copy-start(s32[8,8]{1,0:T(8,128)} %keep.1) | copy-start | bytes 772

commit v2 on v1

--- a/solution.py
+++ b/solution.py
@@ -12,8 +12,8 @@
 MESH = pl.DeviceIdType.MESH
 
 
-def kernel(grid, density, pattern, keep, out, left, right, total, *sems):
-    (left_send, left_recv, up_send, down_send, right_recv, sib_send, sib_recv) = sems
+def kernel(grid, density, pattern_ref, keep_ref, out, left, right, total, pattern, keep, *sems):
+    (left_send, left_recv, up_send, down_send, right_recv, sib_send, sib_recv, load) = sems
     row = lax.axis_index("row")
     col = lax.axis_index("col")
     layer = lax.axis_index("depth")
@@ -24,6 +24,15 @@
     half_blocks = half // BS
     piece = half // PIECES
 
+    loads = [
+        pltpu.make_async_copy(density.at[pl.ds(side * half, half)], right.at[row, side], load.at[side])
+        for side in range(2)
+    ]
+    loads.append(pltpu.make_async_copy(pattern_ref, pattern, load.at[2]))
+    loads.append(pltpu.make_async_copy(keep_ref, keep, load.at[3]))
+    for copy in loads:
+        copy.start()
+
     barrier = pltpu.get_barrier_semaphore()
 
     def greet(device):
@@ -41,14 +50,15 @@
     def _():
         greet((row + 1, col, layer))
 
+    for copy in loads:
+        copy.wait()
     for i in range(blocks):
         for j in range(blocks):
             stored = pattern[row * blocks + i, col * blocks + j] == 1
-            block = density[i * BS:(i + 1) * BS, j * BS:(j + 1) * BS]
             side, at = divmod(i, half_blocks)
-            right[row, side, at * BS:(at + 1) * BS, j * BS:(j + 1) * BS] = jnp.where(
-                stored, block, jnp.zeros_like(block)
-            )
+            rows, cols = slice(at * BS, (at + 1) * BS), slice(j * BS, (j + 1) * BS)
+            block = right[row, side, rows, cols]
+            right[row, side, rows, cols] = jnp.where(stored, block, jnp.zeros_like(block))
 
     ends = (row > 0).astype(jnp.int32) + (row < grid - 1).astype(jnp.int32)
     pl.semaphore_wait(barrier, grid + ends)
@@ -192,15 +202,17 @@
         functools.partial(kernel, grid),
         out_shape=jax.ShapeDtypeStruct((half, tile), jnp.bfloat16),
         in_specs=[
-            pl.BlockSpec(memory_space=pltpu.VMEM),
-            pl.BlockSpec(memory_space=pltpu.SMEM),
-            pl.BlockSpec(memory_space=pltpu.SMEM),
+            pl.BlockSpec(memory_space=pltpu.HBM),
+            pl.BlockSpec(memory_space=pltpu.HBM),
+            pl.BlockSpec(memory_space=pltpu.HBM),
         ],
         out_specs=pl.BlockSpec(memory_space=pltpu.VMEM),
         scratch_shapes=[
             pltpu.VMEM((grid, half, tile), jnp.bfloat16),
             pltpu.VMEM((grid, 2, half, tile), jnp.bfloat16),
             pltpu.VMEM((half, tile), jnp.float32),
+            pltpu.SMEM(pattern.shape, pattern.dtype),
+            pltpu.SMEM(filter_pattern.shape, filter_pattern.dtype),
             dma((grid,)),
             dma((grid,)),
             dma((grid, PIECES)),
@@ -208,6 +220,7 @@
             dma((grid, PIECES)),
             dma((grid, PIECES)),
             dma((grid, PIECES)),
+            dma((4,)),
         ],
         compiler_params=pltpu.CompilerParams(
             collective_id=0, has_side_effects=True, vmem_limit_bytes=40 * 1024 * 1024

time: 29.3 us -> 28.7 us (0.980)
  Pallas kernels: 25.7 us -> 25.1 us
    pallas_call x1, Pallas kernels: 25.7 us -> 25.1 us  [local(): pl.pallas_call(functools.partial(kernel, grid), out_shape=jax.ShapeDtypeS...]
where the time goes in v2:
time: 28.7 us; the launch traced here: 28.2 us
  Pallas kernels  25.1 us (87%)
  local copies, waits for them, and re-layouts  3.12 us (11%)
    pallas_call x1, Pallas kernels, local(): pl.pallas_call(functools.partial(kernel, grid), out_shape=jax.ShapeDtypeS...  25.1 us
    unnamed x7, local copies, waits for them, and re-layouts  3.12 us

profile of v2, /device:TPU:0, one launch (start us, length us, event | category | flops | bytes accessed | tf_op | source)
XLA Modules:
  0.0 28.2 jit_solution(7206799839052316917)
XLA Ops:
  0.0 0.0 copy-start
  0.0 1.0 %copy-done = bf16[512,512]{1,0:T(8,128)(2,1)S(1)} copy-done((bf16[512,512]{1,0:T(8,128)(2,1)S(1)}, bf16[512,512]{1,0:T(8,128)(2,1)}, u32[]{:S(2)}) %copy-start) | copy-done | bytes 524312
  1.0 0.0 copy-start.1
  1.0 0.7 %copy-done.1 = s32[8,8]{1,0:T(8,128)S(1)} copy-done((s32[8,8]{1,0:T(8,128)S(1)}, s32[8,8]{1,0:T(8,128)}, u32[]{:S(2)}) %copy-start.1) | copy-done | bytes 280
  1.7 0.0 copy-start.2
  1.7 0.7 %copy-done.2 = s32[8,8]{1,0:T(8,128)S(1)} copy-done((s32[8,8]{1,0:T(8,128)S(1)}, s32[8,8]{1,0:T(8,128)}, u32[]{:S(2)}) %copy-start.2) | copy-done | bytes 280
  2.4 25.1 %shard_map.37 = bf16[256,512]{1,0:T(8,128)(2,1)S(1)} custom-call(bf16[512,512]{1,0:T(8,128)(2,1)S(1)} %copy-done, s32[8,8]{1,0:T(8,128)S(1)} %copy-done.1, s32[8,8]{1,0:T(8,128)S(1)} %copy-done.2), custom_call_target="tpu_custom_call" | custom-call | tf_op jit(solution)/shard_map/pallas_call | solution.py:201
  27.5 0.7 %copy.5 = bf16[256,512]{1,0:T(8,128)(2,1)} copy(bf16[256,512]{1,0:T(8,128)(2,1)S(1)} %shard_map.37) | data formatting | bytes 524288
Async XLA Ops:
  0.0 1.0 %copy-start = (bf16[512,512]{1,0:T(8,128)(2,1)S(1)}, bf16[512,512]{1,0:T(8,128)(2,1)}, u32[]{:S(2)}) copy-start(bf16[512,512]{1,0:T(8,128)(2,1)} %density.1) | copy-start | bytes 1572868
  1.0 0.7 %copy-start.1 = (s32[8,8]{1,0:T(8,128)S(1)}, s32[8,8]{1,0:T(8,128)}, u32[]{:S(2)}) copy-start(s32[8,8]{1,0:T(8,128)} %pattern_ref.1) | copy-start | bytes 772
  1.7 0.7 %copy-start.2 = (s32[8,8]{1,0:T(8,128)S(1)}, s32[8,8]{1,0:T(8,128)}, u32[]{:S(2)}) copy-start(s32[8,8]{1,0:T(8,128)} %keep_ref.1) | copy-start | bytes 772

commit v3 on v2

--- a/solution.py
+++ b/solution.py
@@ -223,7 +223,7 @@
             dma((4,)),
         ],
         compiler_params=pltpu.CompilerParams(
-            collective_id=0, has_side_effects=True, vmem_limit_bytes=40 * 1024 * 1024
+            collective_id=0, has_side_effects=True, vmem_limit_bytes=63 * 1024 * 1024
         ),
     )(density, pattern, filter_pattern)
 

time: 28.7 us -> 27.8 us (0.969)
  local copies, waits for them, and re-layouts: 3.12 us -> 1.67 us
  Pallas kernels: 25.1 us -> 25.7 us
    unnamed x7 -> x1, local copies, waits for them, and re-layouts: 3.12 us -> 1.67 us
    pallas_call x1, Pallas kernels: 25.1 us -> 25.7 us  [local(): pl.pallas_call(functools.partial(kernel, grid), out_shape=jax.ShapeDtypeS...]
where the time goes in v3:
time: 27.8 us; the launch traced here: 27.4 us
  Pallas kernels  25.7 us (92%)
  local copies, waits for them, and re-layouts  1.67 us (6%)
    pallas_call x1, Pallas kernels, local(): pl.pallas_call(functools.partial(kernel, grid), out_shape=jax.ShapeDtypeS...  25.7 us
    unnamed x1, local copies, waits for them, and re-layouts  1.67 us

profile of v3, /device:TPU:0, one launch (start us, length us, event | category | flops | bytes accessed | tf_op | source)
XLA Modules:
  0.0 27.4 jit_solution(7538311974301410527)
XLA Ops:
  0.0 25.7 %shard_map.37 = bf16[256,512]{1,0:T(8,128)(2,1)} custom-call(bf16[512,512]{1,0:T(8,128)(2,1)} %density.1, s32[8,8]{1,0:T(8,128)} %pattern_ref.1, s32[8,8]{1,0:T(8,128)} %keep_ref.1), custom_call_target="tpu_custom_call" | custom-call | tf_op jit(solution)/shard_map/pallas_call | solution.py:201
  25.7 1.7 %copy.5 = bf16[256,512]{1,0:T(8,128)(2,1)} copy(bf16[256,512]{1,0:T(8,128)(2,1)} %shard_map.37) | data formatting | bytes 524288

commit v4 on v3

v4 whole, which is shorter than its diff:
```python
import functools

import jax
import jax.numpy as jnp
from jax import lax
from jax.experimental import pallas as pl
from jax.experimental.pallas import tpu as pltpu
from jax.sharding import PartitionSpec as P

BS = 256
PIECES = 2
MESH = pl.DeviceIdType.MESH


def goes_up(n, k, c):
    d = lax.rem(c - k + n, n)
    near = (d > 0) & (2 * d < n)
    return (k == c) | (c == n - 1) | near | ((2 * d == n) & (k > 0)) | (2 * (c - k) > n)


def goes_down(n, k, c):
    return goes_up(n, n - 1 - k, n - 1 - c)


def by_chain(n, r, k, c):
    moves = ((k < r) & goes_up(n, k, c)) | ((k > r) & goes_down(n, k, c))
    return (r != c) & moves


def kernel(n, density, pattern_ref, keep_ref, out, left, right, total, pattern, keep, *sems):
    (left_send, pass_send, left_recv, up_send, down_send, extra_send, right_recv,
     sib_send, sib_recv, load) = sems
    row = lax.axis_index("row")
    col = lax.axis_index("col")
    layer = lax.axis_index("depth")
    other = 1 - layer
    tile = density.shape[0]
    blocks = tile // BS
    half = tile // 2
    half_blocks = half // BS
    piece = half // PIECES
    wide = max(w for w in range(1, n + 1) if n % w == 0 and w * w <= n)
    tall = n // wide
    my_y, my_x = lax.div(col, wide), lax.rem(col, wide)

    loads = [
        pltpu.make_async_copy(density.at[pl.ds(side * half, half)], right.at[row, side], load.at[side])
        for side in range(2)
    ]
    loads.append(pltpu.make_async_copy(pattern_ref, pattern, load.at[2]))
    loads.append(pltpu.make_async_copy(keep_ref, keep, load.at[3]))
    for copy in loads:
        copy.start()

    barrier = pltpu.get_barrier_semaphore()

    def greet(device):
        pl.semaphore_signal(barrier, inc=1, device_id=device, device_id_type=MESH)

    for step in range(1, n):
        greet((row, lax.rem(col + step, n), layer))
    greet((row, col, other))

    @pl.when(row > 0)
    def _():
        greet((row - 1, col, layer))

    @pl.when(row < n - 1)
    def _():
        greet((row + 1, col, layer))

    for copy in loads:
        copy.wait()
    for i in range(blocks):
        for j in range(blocks):
            stored = pattern[row * blocks + i, col * blocks + j] == 1
            side, at = divmod(i, half_blocks)
            rows, cols = slice(at * BS, (at + 1) * BS), slice(j * BS, (j + 1) * BS)
            block = right[row, side, rows, cols]
            right[row, side, rows, cols] = jnp.where(stored, block, jnp.zeros_like(block))

    ends = (row > 0).astype(jnp.int32) + (row < n - 1).astype(jnp.int32)
    pl.semaphore_wait(barrier, n + ends)

    up_open = (row < n - 1) & ((col != n - 1) | (row != n - 2))
    down_open = (row > 0) & ((col != 0) | (row != 1))
    corner = row == col

    def part(k, side, p):
        return right.at[k, side, pl.ds(p * piece, piece)]

    def left_part(k, p):
        return left.at[k, pl.ds(p * piece, piece)]

    def remote(src, dst, send, recv, device):
        return pltpu.make_async_remote_copy(
            src, dst, send, recv, device_id=device, device_id_type=MESH
        )

    def upward(k, p):
        ref = part(k, layer, p)
        return remote(ref, ref, up_send.at[k, p], right_recv.at[k, p], (row + 1, col, layer))

    def downward(k, p):
        ref = part(k, layer, p)
        return remote(ref, ref, down_send.at[k, p], right_recv.at[k, p], (row - 1, col, layer))

    def extra(k, p):
        return remote(
            part(k, layer, p), part(col, layer, p),
            extra_send.at[k, p], right_recv.at[col, p], (row, k, layer),
        )

    def arrived(k, p):
        return remote(
            part(k, layer, p), part(k, layer, p),
            extra_send.at[k, p], right_recv.at[k, p], (row, col, other),
        )

    def across(k, p):
        ref = part(k, layer, p)
        return remote(ref, ref, sib_send.at[k, p], sib_recv.at[k, p], (row, col, other))

    def left_across(k, p):
        return remote(
            left_part(k, p), part(k, layer, p),
            sib_send.at[k, p], sib_recv.at[k, p], (row, col, other),
        )

    def from_across(k, p):
        ref = part(k, other, p)
        return remote(ref, ref, sib_send.at[k, p], sib_recv.at[k, p], (row, col, other))

    def along(target, p):
        return remote(
            part(row, layer, p), left_part(col, p),
            left_send.at[target, p], left_recv.at[col, p], (row, target, layer),
        )

    def relay(k, target, slot, p):
        return remote(
            left_part(k, p), left_part(k, p),
            pass_send.at[k, slot, p], left_recv.at[k, p], (row, target, layer),
        )

    beside = [my_y * wide + lax.rem(my_x + i, wide) for i in range(1, wide)]
    above = [lax.rem(my_y + i, tall) * wide + my_x for i in range(1, tall)]
    diagonal = [
        lax.rem(my_y + i, tall) * wide + lax.rem(my_x + j, wide)
        for i in range(1, tall) for j in range(1, wide)
    ]

    def is_even(k):
        return lax.rem(lax.div(k, wide) + lax.rem(k, wide), 2) == 0

    for p in range(PIECES):
        @pl.when(up_open & goes_up(n, row, col))
        def _():
            upward(row, p).start()

        @pl.when(down_open & goes_down(n, row, col))
        def _():
            downward(row, p).start()

        for target in beside + above:
            along(target, p).start()

    left[col] = right[row, layer]
    total[...] = jnp.zeros_like(total)

    def take_left(k, p):
        left_copy = relay(k, col, 0, p)
        left_copy.wait_recv()

        @pl.when(corner)
        def _():
            left_across(k, p).start()

    def take_near(p):
        for k in beside:
            take_left(k, p)

            @pl.when(is_even(k))
            def _():
                for slot, target in enumerate(above):
                    relay(k, target, slot, p).start()

        for k in above:
            take_left(k, p)

            @pl.when(jnp.logical_not(is_even(k)))
            def _():
                for slot, target in enumerate(beside):
                    relay(k, target, slot, p).start()

    def hand_on(k, p):
        @pl.when(by_chain(n, row, k, col))
        def _():
            @pl.when(jnp.logical_not(by_chain(n, row, col, k)))
            def _():
                extra(k, p).start()

            across(k, p).start()

    def pass_on(step, p):
        @pl.when((row >= step) & goes_up(n, row - step, col) & ((col != n - 1) | (row != n - 1)))
        def _():
            k = row - step
            upward(k, p).wait_recv()

            @pl.when(up_open)
            def _():
                upward(k, p).start()

            hand_on(k, p)

        @pl.when((row + step < n) & goes_down(n, row + step, col) & ((col != 0) | (row != 0)))
        def _():
            k = row + step
            downward(k, p).wait_recv()

            @pl.when(down_open)
            def _():
                downward(k, p).start()

            hand_on(k, p)

    def has_extra(k):
        return (k != row) & (k != col) & (row != col) & jnp.logical_not(by_chain(n, row, k, col))

    def take_extra(step):
        @pl.when(lax.abs(row - col) == step)
        def _():
            for p in range(PIECES):
                for k in range(n):
                    @pl.when(has_extra(k))
                    def _():
                        arrived(k, p).wait_recv()
                        across(k, p).start()

    turned = (((1,), (1,)), ((), ()))

    def product(k, ref):
        return lax.dot_general(left[k], ref[...], turned, preferred_element_type=jnp.float32)

    def multiply(k):
        as_is = (k == row) | by_chain(n, row, k, col)

        @pl.when(as_is)
        def _():
            for side in range(2):
                total[...] += jnp.dot(
                    left[k, :, side * half:(side + 1) * half], right[k, side],
                    preferred_element_type=jnp.float32,
                )

        @pl.when(jnp.logical_not(as_is) & jnp.logical_not(corner))
        def _():
            for side in range(2):
                total[:, side * half:(side + 1) * half] += product(k, right.at[k, side])

        @pl.when(jnp.logical_not(as_is) & corner)
        def _():
            total[:, pl.ds(pl.multiple_of(layer * half, half), half)] += product(k, left.at[k])
            total[:, pl.ds(pl.multiple_of(other * half, half), half)] += product(k, right.at[k, other])

    for p in range(PIECES):
        pass_on(1, p)
        take_near(p)
    for step in range(2, n):
        for p in range(PIECES):
            pass_on(step, p)
        if step == 2:
            for p in range(PIECES):
                for k in diagonal:
                    take_left(k, p)
            multiply(row)
        take_extra(step - 1)
    take_extra(n - 1)

    @pl.loop(1, n)
    def _(step):
        k = lax.rem(row + step, n)
        for p in range(PIECES):
            from_across(k, p).wait_recv()
        multiply(k)

    for i in range(half_blocks):
        for j in range(blocks):
            kept = keep[row * blocks + layer * half_blocks + i, col * blocks + j] == 1
            rows, cols = slice(i * BS, (i + 1) * BS), slice(j * BS, (j + 1) * BS)
            value = total[rows, cols]
            out[rows, cols] = jnp.where(kept, value, jnp.zeros_like(value)).astype(out.dtype)

    for p in range(PIECES):
        for target in beside + above:
            along(target, p).wait_send()
        for k in beside:
            @pl.when(is_even(k))
            def _():
                for slot, target in enumerate(above):
                    relay(k, target, slot, p).wait_send()

        for k in above:
            @pl.when(jnp.logical_not(is_even(k)))
            def _():
                for slot, target in enumerate(beside):
                    relay(k, target, slot, p).wait_send()

        for k in range(n):
            @pl.when(up_open & (k <= row) & goes_up(n, k, col))
            def _():
                upward(k, p).wait_send()

            @pl.when(down_open & (k >= row) & goes_down(n, k, col))
            def _():
                downward(k, p).wait_send()

            @pl.when(k != row)
            def _():
                across(k, p).wait_send()

            @pl.when(by_chain(n, row, k, col) & jnp.logical_not(by_chain(n, row, col, k)))
            def _():
                extra(k, p).wait_send()


def local(density, pattern, filter_pattern):
    grid = lax.axis_size("row")
    tile = density.shape[0]
    half = tile // 2
    dma = pltpu.SemaphoreType.DMA
    return pl.pallas_call(
        functools.partial(kernel, grid),
        out_shape=jax.ShapeDtypeStruct((half, tile), jnp.bfloat16),
        in_specs=[
            pl.BlockSpec(memory_space=pltpu.HBM),
            pl.BlockSpec(memory_space=pltpu.HBM),
            pl.BlockSpec(memory_space=pltpu.HBM),
        ],
        out_specs=pl.BlockSpec(memory_space=pltpu.VMEM),
        scratch_shapes=[
            pltpu.VMEM((grid, half, tile), jnp.bfloat16),
            pltpu.VMEM((grid, 2, half, tile), jnp.bfloat16),
            pltpu.VMEM((half, tile), jnp.float32),
            pltpu.SMEM(pattern.shape, pattern.dtype),
            pltpu.SMEM(filter_pattern.shape, filter_pattern.dtype),
            dma((grid, PIECES)),
            dma((grid, grid, PIECES)),
            dma((grid, PIECES)),
            dma((grid, PIECES)),
            dma((grid, PIECES)),
            dma((grid, PIECES)),
            dma((grid, PIECES)),
            dma((grid, PIECES)),
            dma((grid, PIECES)),
            dma((4,)),
        ],
        compiler_params=pltpu.CompilerParams(
            collective_id=0, has_side_effects=True, vmem_limit_bytes=63 * 1024 * 1024
        ),
    )(density, pattern, filter_pattern)


def solution(mesh):
    return jax.shard_map(
        local,
        mesh=mesh,
        in_specs=(P("row", "col"), P(), P()),
        out_specs=P(("row", "depth"), "col"),
        check_vma=False,
    )
```

time: 27.8 us -> 30.1 us (1.083)
  the two profiles are of different devices: /device:TPU:0 before, /device:TPU:7 now
where the time goes in v4:
time: 30.1 us; the launch traced here: 30 us
  Pallas kernels  28.3 us (94%)
  local copies, waits for them, and re-layouts  1.67 us (6%)
    pallas_call x1, Pallas kernels, local(): pl.pallas_call(functools.partial(kernel, grid), out_shape=jax.ShapeDtypeS...  28.3 us
    unnamed x1, local copies, waits for them, and re-layouts  1.67 us

profile of v4, /device:TPU:7, one launch (start us, length us, event | category | flops | bytes accessed | tf_op | source)
XLA Modules:
  0.0 30.0 jit_solution(9478357281812528929)
XLA Ops:
  0.0 28.3 %shard_map.37 = bf16[256,512]{1,0:T(8,128)(2,1)} custom-call(bf16[512,512]{1,0:T(8,128)(2,1)} %density.1, s32[8,8]{1,0:T(8,128)} %pattern_ref.1, s32[8,8]{1,0:T(8,128)} %keep_ref.1), custom_call_target="tpu_custom_call" | custom-call | tf_op jit(solution)/shard_map/pallas_call | solution.py:333
  28.3 1.7 %copy.5 = bf16[256,512]{1,0:T(8,128)(2,1)} copy(bf16[256,512]{1,0:T(8,128)(2,1)} %shard_map.37) | data formatting | bytes 524288

commit v5 on v4

--- a/solution.py
+++ b/solution.py
@@ -8,7 +8,7 @@
 from jax.sharding import PartitionSpec as P
 
 BS = 256
-PIECES = 2
+PIECES = 4
 MESH = pl.DeviceIdType.MESH
 
 
@@ -25,6 +25,17 @@
 def by_chain(n, r, k, c):
     moves = ((k < r) & goes_up(n, k, c)) | ((k > r) & goes_down(n, k, c))
     return (r != c) & moves
+
+
+def is_late(n, k, c):
+    from_below = (k >= 2) & goes_up(n, k - 2, c)
+    return (k >= 1) & goes_up(n, k, c) & goes_up(n, k - 1, c) & jnp.logical_not(from_below)
+
+
+def tile_at(n, step, r, c):
+    k = r - step
+    early = jnp.where(is_late(n, k, c), k - 1, k)
+    return jnp.where(is_late(n, k + 1, c), k + 1, early) if step > 1 else early
 
 
 def kernel(n, density, pattern_ref, keep_ref, out, left, right, total, pattern, keep, *sems):
@@ -85,6 +96,8 @@
     up_open = (row < n - 1) & ((col != n - 1) | (row != n - 2))
     down_open = (row > 0) & ((col != 0) | (row != 1))
     corner = row == col
+    late_up = is_late(n, row, col)
+    late_down = is_late(n, n - 1 - row, n - 1 - col)
 
     def part(k, side, p):
         return right.at[k, side, pl.ds(p * piece, piece)]
@@ -154,11 +167,11 @@
         return lax.rem(lax.div(k, wide) + lax.rem(k, wide), 2) == 0
 
     for p in range(PIECES):
-        @pl.when(up_open & goes_up(n, row, col))
+        @pl.when(up_open & goes_up(n, row, col) & ((p == 0) | jnp.logical_not(late_up)))
         def _():
             upward(row, p).start()
 
-        @pl.when(down_open & goes_down(n, row, col))
+        @pl.when(down_open & goes_down(n, row, col) & ((p == 0) | jnp.logical_not(late_down)))
         def _():
             downward(row, p).start()
 
@@ -202,10 +215,11 @@
 
             across(k, p).start()
 
-    def pass_on(step, p):
-        @pl.when((row >= step) & goes_up(n, row - step, col) & ((col != n - 1) | (row != n - 1)))
-        def _():
-            k = row - step
+    def pass_up(step, p):
+        k = tile_at(n, step, row, col)
+
+        @pl.when((k >= 0) & goes_up(n, k, col) & ((col != n - 1) | (row != n - 1)))
+        def _():
             upward(k, p).wait_recv()
 
             @pl.when(up_open)
@@ -214,9 +228,11 @@
 
             hand_on(k, p)
 
-        @pl.when((row + step < n) & goes_down(n, row + step, col) & ((col != 0) | (row != 0)))
-        def _():
-            k = row + step
+    def pass_down(step, p):
+        k = n - 1 - tile_at(n, step, n - 1 - row, n - 1 - col)
+
+        @pl.when((k < n) & goes_down(n, k, col) & ((col != 0) | (row != 0)))
+        def _():
             downward(k, p).wait_recv()
 
             @pl.when(down_open)
@@ -224,6 +240,17 @@
                 downward(k, p).start()
 
             hand_on(k, p)
+
+    def send_late():
+        @pl.when(up_open & goes_up(n, row, col) & late_up)
+        def _():
+            for p in range(1, PIECES):
+                upward(row, p).start()
+
+        @pl.when(down_open & goes_down(n, row, col) & late_down)
+        def _():
+            for p in range(1, PIECES):
+                downward(row, p).start()
 
     def has_extra(k):
         return (k != row) & (k != col) & (row != col) & jnp.logical_not(by_chain(n, row, k, col))
@@ -265,11 +292,15 @@
             total[:, pl.ds(pl.multiple_of(other * half, half), half)] += product(k, right.at[k, other])
 
     for p in range(PIECES):
-        pass_on(1, p)
+        pass_up(1, p)
+        pass_down(1, p)
+        if p == PIECES - 1:
+            send_late()
         take_near(p)
     for step in range(2, n):
         for p in range(PIECES):
-            pass_on(step, p)
+            pass_up(step, p)
+            pass_down(step, p)
         if step == 2:
             for p in range(PIECES):
                 for k in diagonal:

time: 30.1 us -> 30.1 us (level)
  the two profiles are of different devices: /device:TPU:7 before, /device:TPU:5 now
where the time goes in v5:
time: 30.1 us; the launch traced here: 30 us
  Pallas kernels  28.3 us (94%)
  local copies, waits for them, and re-layouts  1.67 us (6%)
    pallas_call x1, Pallas kernels, local(): pl.pallas_call(functools.partial(kernel, grid), out_shape=jax.ShapeDtypeS...  28.3 us
    unnamed x1, local copies, waits for them, and re-layouts  1.67 us

profile of v5, /device:TPU:5, one launch (start us, length us, event | category | flops | bytes accessed | tf_op | source)
XLA Modules:
  0.0 30.0 jit_solution(210069543538264198)
XLA Ops:
  0.0 28.3 %shard_map.37 = bf16[256,512]{1,0:T(8,128)(2,1)} custom-call(bf16[512,512]{1,0:T(8,128)(2,1)} %density.1, s32[8,8]{1,0:T(8,128)} %pattern_ref.1, s32[8,8]{1,0:T(8,128)} %keep_ref.1), custom_call_target="tpu_custom_call" | custom-call | tf_op jit(solution)/shard_map/pallas_call | solution.py:364
  28.3 1.7 %copy.5 = bf16[256,512]{1,0:T(8,128)(2,1)} copy(bf16[256,512]{1,0:T(8,128)(2,1)} %shard_map.37) | data formatting | bytes 524288

commit v6 on v4

--- a/solution.py
+++ b/solution.py
@@ -12,23 +12,8 @@
 MESH = pl.DeviceIdType.MESH
 
 
-def goes_up(n, k, c):
-    d = lax.rem(c - k + n, n)
-    near = (d > 0) & (2 * d < n)
-    return (k == c) | (c == n - 1) | near | ((2 * d == n) & (k > 0)) | (2 * (c - k) > n)
-
-
-def goes_down(n, k, c):
-    return goes_up(n, n - 1 - k, n - 1 - c)
-
-
-def by_chain(n, r, k, c):
-    moves = ((k < r) & goes_up(n, k, c)) | ((k > r) & goes_down(n, k, c))
-    return (r != c) & moves
-
-
 def kernel(n, density, pattern_ref, keep_ref, out, left, right, total, pattern, keep, *sems):
-    (left_send, pass_send, left_recv, up_send, down_send, extra_send, right_recv,
+    (left_send, pass_send, left_recv, up_send, down_send, right_recv,
      sib_send, sib_recv, load) = sems
     row = lax.axis_index("row")
     col = lax.axis_index("col")
@@ -105,18 +90,6 @@
         ref = part(k, layer, p)
         return remote(ref, ref, down_send.at[k, p], right_recv.at[k, p], (row - 1, col, layer))
 
-    def extra(k, p):
-        return remote(
-            part(k, layer, p), part(col, layer, p),
-            extra_send.at[k, p], right_recv.at[col, p], (row, k, layer),
-        )
-
-    def arrived(k, p):
-        return remote(
-            part(k, layer, p), part(k, layer, p),
-            extra_send.at[k, p], right_recv.at[k, p], (row, col, other),
-        )
-
     def across(k, p):
         ref = part(k, layer, p)
         return remote(ref, ref, sib_send.at[k, p], sib_recv.at[k, p], (row, col, other))
@@ -154,11 +127,11 @@
         return lax.rem(lax.div(k, wide) + lax.rem(k, wide), 2) == 0
 
     for p in range(PIECES):
-        @pl.when(up_open & goes_up(n, row, col))
+        @pl.when(up_open)
         def _():
             upward(row, p).start()
 
-        @pl.when(down_open & goes_down(n, row, col))
+        @pl.when(down_open)
         def _():
             downward(row, p).start()
 
@@ -193,17 +166,8 @@
                 for slot, target in enumerate(beside):
                     relay(k, target, slot, p).start()
 
-    def hand_on(k, p):
-        @pl.when(by_chain(n, row, k, col))
-        def _():
-            @pl.when(jnp.logical_not(by_chain(n, row, col, k)))
-            def _():
-                extra(k, p).start()
-
-            across(k, p).start()
-
     def pass_on(step, p):
-        @pl.when((row >= step) & goes_up(n, row - step, col) & ((col != n - 1) | (row != n - 1)))
+        @pl.when((row >= step) & ((col != n - 1) | (row != n - 1)))
         def _():
             k = row - step
             upward(k, p).wait_recv()
@@ -212,9 +176,11 @@
             def _():
                 upward(k, p).start()
 
-            hand_on(k, p)
-
-        @pl.when((row + step < n) & goes_down(n, row + step, col) & ((col != 0) | (row != 0)))
+            @pl.when(jnp.logical_not(corner))
+            def _():
+                across(k, p).start()
+
+        @pl.when((row + step < n) & ((col != 0) | (row != 0)))
         def _():
             k = row + step
             downward(k, p).wait_recv()
@@ -223,20 +189,9 @@
             def _():
                 downward(k, p).start()
 
-            hand_on(k, p)
-
-    def has_extra(k):
-        return (k != row) & (k != col) & (row != col) & jnp.logical_not(by_chain(n, row, k, col))
-
-    def take_extra(step):
-        @pl.when(lax.abs(row - col) == step)
-        def _():
-            for p in range(PIECES):
-                for k in range(n):
-                    @pl.when(has_extra(k))
-                    def _():
-                        arrived(k, p).wait_recv()
-                        across(k, p).start()
+            @pl.when(jnp.logical_not(corner))
+            def _():
+                across(k, p).start()
 
     turned = (((1,), (1,)), ((), ()))
 
@@ -244,7 +199,7 @@
         return lax.dot_general(left[k], ref[...], turned, preferred_element_type=jnp.float32)
 
     def multiply(k):
-        as_is = (k == row) | by_chain(n, row, k, col)
+        as_is = (k == row) | jnp.logical_not(corner)
 
         @pl.when(as_is)
         def _():
@@ -254,12 +209,7 @@
                     preferred_element_type=jnp.float32,
                 )
 
-        @pl.when(jnp.logical_not(as_is) & jnp.logical_not(corner))
-        def _():
-            for side in range(2):
-                total[:, side * half:(side + 1) * half] += product(k, right.at[k, side])
-
-        @pl.when(jnp.logical_not(as_is) & corner)
+        @pl.when(jnp.logical_not(as_is))
         def _():
             total[:, pl.ds(pl.multiple_of(layer * half, half), half)] += product(k, left.at[k])
             total[:, pl.ds(pl.multiple_of(other * half, half), half)] += product(k, right.at[k, other])
@@ -275,8 +225,6 @@
                 for k in diagonal:
                     take_left(k, p)
             multiply(row)
-        take_extra(step - 1)
-    take_extra(n - 1)
 
     @pl.loop(1, n)
     def _(step):
@@ -308,21 +256,17 @@
                     relay(k, target, slot, p).wait_send()
 
         for k in range(n):
-            @pl.when(up_open & (k <= row) & goes_up(n, k, col))
+            @pl.when(up_open & (k <= row))
             def _():
                 upward(k, p).wait_send()
 
-            @pl.when(down_open & (k >= row) & goes_down(n, k, col))
+            @pl.when(down_open & (k >= row))
             def _():
                 downward(k, p).wait_send()
 
             @pl.when(k != row)
             def _():
                 across(k, p).wait_send()
-
-            @pl.when(by_chain(n, row, k, col) & jnp.logical_not(by_chain(n, row, col, k)))
-            def _():
-                extra(k, p).wait_send()
 
 
 def local(density, pattern, filter_pattern):
@@ -353,7 +297,6 @@
             dma((grid, PIECES)),
             dma((grid, PIECES)),
             dma((grid, PIECES)),
-            dma((grid, PIECES)),
             dma((4,)),
         ],
         compiler_params=pltpu.CompilerParams(

time: 30.1 us -> 26.1 us (0.87)
  the two profiles are of different devices: /device:TPU:7 before, /device:TPU:25 now
where the time goes in v6:
time: 26.1 us; the launch traced here: 25.9 us
  Pallas kernels  24.2 us (93%)
  local copies, waits for them, and re-layouts  1.67 us (6%)
    pallas_call x1, Pallas kernels, local(): pl.pallas_call(functools.partial(kernel, grid), out_shape=jax.ShapeDtypeS...  24.2 us
    unnamed x1, local copies, waits for them, and re-layouts  1.67 us

profile of v6, /device:TPU:25, one launch (start us, length us, event | category | flops | bytes accessed | tf_op | source)
XLA Modules:
  0.0 25.9 jit_solution(17090281645510338744)
XLA Ops:
  0.0 24.2 %shard_map.37 = bf16[256,512]{1,0:T(8,128)(2,1)} custom-call(bf16[512,512]{1,0:T(8,128)(2,1)} %density.1, s32[8,8]{1,0:T(8,128)} %pattern_ref.1, s32[8,8]{1,0:T(8,128)} %keep_ref.1), custom_call_target="tpu_custom_call" | custom-call | tf_op jit(solution)/shard_map/pallas_call | solution.py:277
  24.2 1.7 %copy.5 = bf16[256,512]{1,0:T(8,128)(2,1)} copy(bf16[256,512]{1,0:T(8,128)(2,1)} %shard_map.37) | data formatting | bytes 524288

commit v7 on v6

--- a/solution.py
+++ b/solution.py
@@ -214,6 +214,14 @@
             total[:, pl.ds(pl.multiple_of(layer * half, half), half)] += product(k, left.at[k])
             total[:, pl.ds(pl.multiple_of(other * half, half), half)] += product(k, right.at[k, other])
 
+    def multiply_step(step):
+        for k, there in ((row - step, row >= step), (row + step, row + step < n)):
+            @pl.when(there)
+            def _():
+                for p in range(PIECES):
+                    from_across(k, p).wait_recv()
+                multiply(k)
+
     for p in range(PIECES):
         pass_on(1, p)
         take_near(p)
@@ -225,13 +233,9 @@
                 for k in diagonal:
                     take_left(k, p)
             multiply(row)
-
-    @pl.loop(1, n)
-    def _(step):
-        k = lax.rem(row + step, n)
-        for p in range(PIECES):
-            from_across(k, p).wait_recv()
-        multiply(k)
+        multiply_step(step - 1)
+
+    multiply_step(n - 1)
 
     for i in range(half_blocks):
         for j in range(blocks):

time: 26.1 us -> 25.7 us (0.985)
  the two profiles are of different devices: /device:TPU:25 before, /device:TPU:5 now
where the time goes in v7:
time: 25.7 us; the launch traced here: 25.5 us
  Pallas kernels  23.8 us (93%)
  local copies, waits for them, and re-layouts  1.67 us (6%)
    pallas_call x1, Pallas kernels, local(): pl.pallas_call(functools.partial(kernel, grid), out_shape=jax.ShapeDtypeS...  23.8 us
    unnamed x1, local copies, waits for them, and re-layouts  1.67 us

profile of v7, /device:TPU:5, one launch (start us, length us, event | category | flops | bytes accessed | tf_op | source)
XLA Modules:
  0.0 25.5 jit_solution(7102390950348023196)
XLA Ops:
  0.0 23.8 %shard_map.37 = bf16[256,512]{1,0:T(8,128)(2,1)} custom-call(bf16[512,512]{1,0:T(8,128)(2,1)} %density.1, s32[8,8]{1,0:T(8,128)} %pattern_ref.1, s32[8,8]{1,0:T(8,128)} %keep_ref.1), custom_call_target="tpu_custom_call" | custom-call | tf_op jit(solution)/shard_map/pallas_call | solution.py:281
  23.8 1.7 %copy.5 = bf16[256,512]{1,0:T(8,128)(2,1)} copy(bf16[256,512]{1,0:T(8,128)(2,1)} %shard_map.37) | data formatting | bytes 524288
